TPU v7x, 256 devices: a whole 4x4x8 slice. The times are simulated.
256 devices in a mesh: row: 32 (over z, x_hi, core), col: 8 (over y, x_lo).
Axes of the slice: x: 4 (x_hi: 2, x_lo: 2; x = x_hi * 2 + x_lo), y: 4, z: 8, core: 2. Of those that a mesh axis runs over, the one named last changes fastest.
Arguments:
- density: bfloat16 [12288, 12288], P('col', 'row'), may hold values from -1.5 to 1.5
- block_mask: int32 [96, 96], replicated, may hold values from 0 to 1, as said below
- owner: int32 [4, 8], replicated, may hold values from 0 to 31, as said below
Outputs:
- square_part: float32 [12288, 12288], P('col', 'row')
Inputs may be any that keep to these rules, and one draw needn't show every extreme that they name: owner[t, g] // 4 equals (g + t) mod 8. `block_mask`: each tile of 12 x 3 blocks (block rows g * 12 onward, block columns j * 3 onward) has at most 21 entries equal to 1, and in every draw some tile has exactly 21.
All inputs are finite; a program needn't handle non-finite values.
Results may differ from a plain program's by a relative error of at most 0.0003.
Values may be sent and summed in bfloat16 or wider, within the bound.
A program may use at most 64 MiB of HBM per device.

v0:
```python
import jax
import jax.numpy as jnp
from jax import lax
from jax.sharding import PartitionSpec as P

BLOCK = 128
STEPS = 4


def shifted(x, axis, by):
    devices = lax.axis_size(axis)
    return lax.ppermute(x, axis, [(i, (i + by) % devices) for i in range(devices)])


def from_root(block, axis, source):
    block = jnp.where(lax.axis_index(axis) == source, block, jnp.zeros_like(block))
    return lax.psum(block, axis)


def shards(density, block_mask, owner):
    row_count = lax.axis_size("row")
    col_count = lax.axis_size("col")
    grid_row = lax.axis_index("col")
    grid_col = lax.axis_index("row")
    tile_rows, tile_width = density.shape
    row_blocks = tile_rows // BLOCK
    col_blocks = tile_width // BLOCK
    sub_count = row_count // col_count
    own_mask = lax.dynamic_slice(
        block_mask, (grid_row * row_blocks, grid_col * col_blocks), (row_blocks, col_blocks)
    )
    shaped = density.reshape(row_blocks, BLOCK, col_blocks, BLOCK)
    kept = jnp.where(own_mask[:, None, :, None] == 1, shaped, jnp.zeros((), jnp.bfloat16))
    masked = kept.reshape(tile_rows, tile_width)
    accumulated = jnp.zeros((tile_rows, tile_width), jnp.float32)
    held_tile = masked
    for section_index in range(STEPS):
        root_index = owner[section_index, grid_row]
        slab_index = root_index % sub_count
        if section_index > 0:
            held_tile = shifted(held_tile, "col", -1)
        right_slab = lax.dynamic_slice_in_dim(held_tile, slab_index * tile_width, tile_width, 0)
        left_tile = from_root(masked, "row", root_index)
        accumulated = accumulated + jnp.dot(
            left_tile, right_slab, preferred_element_type=jnp.float32
        )
    return accumulated


def solution(mesh):
    placed = (P("col", "row"), P(), P())
    return jax.shard_map(
        shards, mesh=mesh, in_specs=placed, out_specs=P("col", "row"), check_vma=False
    )
```

profile of v0, /device:TPU:9, one launch (start us, length us, event | category | flops | bytes accessed | tf_op | source)
XLA Modules:
  0.0 320.1 jit_solution(13729653389011136727)
XLA Ops:
  6.5 0.0 all-reduce.3.cloned.1.call-start
  6.5 0.8 dynamic_slice.28
  7.3 0.1 copy.8
  7.4 1.5 constant_dynamic-slice_fusion.1
  9.6 1.6 copy.7
  13.1 0.3 broadcast_in_dim.15
  13.3 1.4 broadcast_select_fusion
  14.7 1.9 broadcast_select_fusion.1
  16.6 0.0 all-reduce.3.cloned.1.call-update
  16.6 1.2 collective-permute-start
  17.8 33.2 %collective-permute-done = bf16[1536,384]{0,1:T(8,128)(2,1)S(1)} collective-permute-done((bf16[1536,384]{0,1:T(8,128)(2,1)S(1)}, bf16[1536,384]{0,1:T(8,128)(2,1)S(1)}, u32[]{:S(2)}, u32[]{:S(2)}) %collective-permute-start) | collective-permute-done | bytes 1179680 | tf_op jit(solution)/shard_map/ppermute | solution.py:12
  51.0 1.7 collective-permute-start.1
  52.7 38.7 %collective-permute-done.1 = bf16[1536,384]{0,1:T(8,128)(2,1)S(1)} collective-permute-done((bf16[1536,384]{0,1:T(8,128)(2,1)S(1)}, bf16[1536,384]{0,1:T(8,128)(2,1)S(1)}, u32[]{:S(2)}, u32[]{:S(2)}) %collective-permute-start.1) | collective-permute-done | bytes 1179680 | tf_op jit(solution)/shard_map/ppermute | solution.py:12
  91.4 4.2 %collective-permute-start.2 = (bf16[1536,384]{0,1:T(8,128)(2,1)S(1)}, bf16[1536,384]{0,1:T(8,128)(2,1)}, u32[]{:S(2)}, u32[]{:S(2)}) collective-permute-start(bf16[1536,384]{0,1:T(8,128)(2,1)S(1)} %collective-permute-done.1), channel_id=1, source_target_pairs={{0,7},{1,0},{2,1},{3,2},{4,3},{5,4},{6,5},{7,6},{8,15},{9,8},{10,9... | collective-permute-start | bytes 3538952 | tf_op jit(solution)/shard_map/ppermute | solution.py:12
  103.4 201.7 %all-reduce.3.cloned.1.call-done = (bf16[1536,384]{0,1:T(8,128)(2,1)}, bf16[1536,384]{0,1:T(8,128)(2,1)}, bf16[1536,384]{0,1:T(8,128)(2,1)}, bf16[1536,384]{0,1:T(8,128)(2,1)}) async-done(((bf16[1536,384]{0,1:T(8,128)(2,1)}, bf16[1536,384]{0,1:T(8,128)(2,1)}, bf16[1536,384]{0,1:T(8,128)(2,1)}, bf16[1536,384]{0,1:T(8,128)(2,1)}), (bf16[1536,384]{0,1:T(8,128)(2,1)}, bf16[1536,384]{0,1:T(8,128)(2,1)}, ...) | async-done | bytes 4718608 | tf_op jit(solution)/shard_map/psum | solution.py:17
  305.1 0.0 copy-start.2
  305.1 2.3 fusion.3
  307.4 0.0 copy-done.2
  307.4 0.0 copy-start.1
  307.4 0.9 convolution_add_fusion.2
  308.3 0.3 copy-done.1
  308.7 0.0 copy-start
  308.7 0.9 convolution_add_fusion.1
  309.6 0.0 collective-permute-done.2
  309.6 0.3 copy-done
  309.9 3.3 %convolution_add_fusion = f32[1536,384]{1,0:T(8,128)} fusion(f32[1536,384]{1,0:T(8,128)S(1)} %convolution_add_fusion.1, bf16[1536,384]{0,1:T(8,128)(2,1)S(1)} %copy-done, bf16[1536,384]{0,1:T(8,128)(2,1)} %collective-permute-done.2, s32[]{:T(128)S(6)} %select_n.93), kind=kOutput, calls=%fused_computation | convolution fusion | flops 453574656 | bytes 6193156 | tf_op jit(solution)/shard_map/dot_general | solution.py:44
  (1 shorter events, 0.0 us)
Async XLA Ops:
  6.5 298.5 %all-reduce.3.cloned.1.call-start = ((), (), s32[]{:S(2)}) async-start(), calls=%async_computation | async-start | bytes 9437184 | tf_op jit(solution)/shard_map/psum | solution.py:17
  16.6 34.3 %collective-permute-start = (bf16[1536,384]{0,1:T(8,128)(2,1)S(1)}, bf16[1536,384]{0,1:T(8,128)(2,1)S(1)}, u32[]{:S(2)}, u32[]{:S(2)}) collective-permute-start(bf16[1536,384]{0,1:T(8,128)(2,1)S(1)} %get-tuple-element.10), channel_id=1, source_target_pairs={{0,7},{1,0},{2,1},{3,2},{4,3},{5,4},{6,5},{7,6},{8,15},{9,8},{10,9... | collective-permute-start | bytes 3538952 | tf_op jit(solution)/shard_map/ppermute | solution.py:12
  51.0 40.4 %collective-permute-start.1 = (bf16[1536,384]{0,1:T(8,128)(2,1)S(1)}, bf16[1536,384]{0,1:T(8,128)(2,1)S(1)}, u32[]{:S(2)}, u32[]{:S(2)}) collective-permute-start(bf16[1536,384]{0,1:T(8,128)(2,1)S(1)} %collective-permute-done), channel_id=1, source_target_pairs={{0,7},{1,0},{2,1},{3,2},{4,3},{5,4},{6,5},{7,6},{8,15},{9,8},{10,9... | collective-permute-start | bytes 3538952 | tf_op jit(solution)/shard_map/ppermute | solution.py:12
  91.4 218.2 %collective-permute-start.2 = (bf16[1536,384]{0,1:T(8,128)(2,1)S(1)}, bf16[1536,384]{0,1:T(8,128)(2,1)}, u32[]{:S(2)}, u32[]{:S(2)}) collective-permute-start(bf16[1536,384]{0,1:T(8,128)(2,1)S(1)} %collective-permute-done.1), channel_id=1, source_target_pairs={{0,7},{1,0},{2,1},{3,2},{4,3},{5,4},{6,5},{7,6},{8,15},{9,8},{10,9... | collective-permute-start | bytes 3538952 | tf_op jit(solution)/shard_map/ppermute | solution.py:12
  305.1 2.3 copy-start.2
  307.4 1.3 copy-start.1
  308.7 1.3 copy-start
Sparse Core Ops, SparseCore 0:
  16.8 288.2 all-reduce.2
where the time goes:
time: 321 us; the launch traced here: 320 us
  waiting for transfers between devices  274 us (85%)
  between operations  23.8 us (7%)
  matrix products  7.54 us (2%)
  starting transfers between devices  7.16 us (2%)
  local copies, waits for them, and re-layouts  4.82 us (2%)
  other arithmetic  3.28 us (1%)
    psum x1, waiting for transfers between devices, from_root(): return lax.psum(block, axis)  202 us
    ppermute x3, waiting for transfers between devices, shifted(): lax.ppermute(x, axis, [(i, (i + by) % devices) for i in range(devices)])  71.8 us
    dot_general x4, matrix products, shards(): jnp.dot(left_tile, right_slab, preferred_element_type=jnp.float32)  7.54 us
    ppermute x3, starting transfers between devices, shifted(): lax.ppermute(x, axis, [(i, (i + by) % devices) for i in range(devices)])  7.16 us
  transfers between devices with their start and end apart: 4, of which 3 were waited for; matrix products, arithmetic and copies ran while one was open for 1% of the time, Pallas kernels for 0%

commit v1 on v0

v1 whole, which is shorter than its diff:
```python
import functools

import jax
import jax.numpy as jnp
from jax import lax
from jax.experimental import pallas as pl
from jax.experimental.pallas import tpu as pltpu
from jax.sharding import PartitionSpec as P

BLOCK = 128
STEPS = 4
CAP = 21
HALF = BLOCK // 2
CHUNKS = 7
SPAN = CAP // CHUNKS
LAG = 3
MESH = pl.DeviceIdType.MESH


def kernel(
    n_row, n_col, density, mask, owner, out,
    tile, nxt, slots, packed, chosen, crossed, near, far, r_send, r_all, wide,
    load_sem, swap_s, swap_r, cross_s, cross_r, up_s, down_s, ring_r, mate_s, mate_r, slab_s, slab_r,
):
    g = lax.axis_index("col")
    j = lax.axis_index("row")
    sub = n_row // n_col
    planes = n_col
    plane = j // sub
    place = lax.rem(j, sub)
    core = lax.rem(place, 2)
    rel = lax.rem(plane - g + planes, planes)
    is_source = rel < STEPS
    row_blocks, _, width = density.shape
    col_blocks = width // BLOCK

    def at_plane(by):
        return {"col": g, "row": lax.rem(plane + by + planes, planes) * sub + place}

    def at_grid_row(by):
        return {"col": lax.rem(g + by + n_col, n_col), "row": j}

    mate = {"col": g, "row": plane * sub + place + 1 - 2 * core}
    across = {"col": g, "row": plane * sub + lax.rem(place + 2, sub)}

    barrier = pltpu.get_barrier_semaphore()
    senders = [mate, across, at_plane(1), at_plane(-1)] + [at_grid_row(t) for t in range(1, STEPS)]
    for device in senders:
        pl.semaphore_signal(barrier, inc=1, device_id=device, device_id_type=MESH)

    loads = [
        pltpu.make_async_copy(
            density.at[:, :, pl.ds(b * BLOCK, BLOCK)], tile.at[b, pl.ds(0, row_blocks)], load_sem.at[b]
        )
        for b in range(col_blocks)
    ]
    for load in loads:
        load.start()
    for b in range(col_blocks):
        tile[b, row_blocks] = jnp.zeros((BLOCK, BLOCK), jnp.bfloat16)
    for t in range(STEPS):
        near[t, CAP] = jnp.zeros((HALF, BLOCK), jnp.bfloat16)
        far[t, CAP] = jnp.zeros((HALF, BLOCK), jnp.bfloat16)

    first = jnp.int32(4 * (row_blocks - 1))
    nxt[4 * row_blocks] = first
    for q in reversed(range(4 * row_blocks)):
        a, b = q // 4, q % 4
        if b < col_blocks:
            bit = mask[g * row_blocks + a, j * col_blocks + b]
            first = first + bit * (q - first)
        nxt[q] = first

    for t in range(STEPS):
        at = owner[t, g] * col_blocks
        count = jnp.int32(0)
        for a in range(row_blocks):
            for b in range(col_blocks):
                bit = mask[g * row_blocks + a, at + b]
                slots[t, a * col_blocks + b] = CAP + bit * (count - CAP)
                count = count + bit

    for load in loads:
        load.wait()

    q = nxt[0]
    for s in range(CAP):
        block = tile[q & 3, q >> 2]
        packed[0, s] = block[:HALF]
        packed[1, s] = block[HALF:]
        q = nxt[q + 1]

    for t in range(STEPS):
        slab = (owner[t, lax.rem(g - t + n_col, n_col)] & (sub - 1)) * col_blocks
        for a in range(col_blocks):
            for b in range(col_blocks):
                bit = mask[g * row_blocks + slab + a, j * col_blocks + b]
                line = row_blocks + bit * (slab + a - row_blocks)
                block = tile[b, line]
                if t == 0:
                    r_all[0, a * BLOCK : (a + 1) * BLOCK, b * BLOCK : (b + 1) * BLOCK] = block
                else:
                    r_send[t - 1, a * BLOCK : (a + 1) * BLOCK, b * BLOCK : (b + 1) * BLOCK] = block

    pl.semaphore_wait(barrier, len(senders))

    def remote(src, dst, send, recv, device):
        return pltpu.make_async_remote_copy(
            src_ref=src, dst_ref=dst, send_sem=send, recv_sem=recv, device_id=device, device_id_type=MESH
        )

    def part(k):
        return pl.ds(k * SPAN, SPAN)

    swap = remote(packed.at[1 - core], packed.at[2], swap_s, swap_r, mate)

    def cross(k):
        return remote(chosen.at[part(k)], crossed.at[part(k)], cross_s.at[k], cross_r.at[k], across)

    def ring(t, k, by, sems):
        return remote(near.at[t, part(k)], near.at[t, part(k)], sems.at[t, k], ring_r.at[t, k], at_plane(by))

    def hand(t, k):
        return remote(near.at[t, part(k)], far.at[t, part(k)], mate_s.at[t, k], mate_r.at[t, k], mate)

    slabs = [
        remote(r_send.at[t - 1], r_all.at[t], slab_s.at[t - 1], slab_r.at[t - 1], at_grid_row(-t))
        for t in range(1, STEPS)
    ]

    pick = owner[jnp.minimum(rel, STEPS - 1), g] & (sub - 1)

    @pl.when(is_source)
    def _():
        swap.start()
        swap.wait_recv()
        kept = core + ((pick + core) & 1) * (2 - core)

        @pl.loop(0, CHUNKS)
        def _(k):
            chosen[part(k)] = packed[kept, part(k)]
            cross(k).start()

    for copy in slabs:
        copy.start()

    def up_reach(t):
        return jnp.where(t < 2, 2, 5)

    def down_reach(t):
        return jnp.where(t < 2, 5, 2)

    moved = ((pick >> 1) + place // 2) & 1
    from_across = jnp.full((SPAN, HALF, BLOCK), moved, jnp.int32).astype(jnp.float32).astype(jnp.bfloat16)

    @pl.loop(0, CHUNKS + 5 * LAG + CHUNKS - LAG)
    def _(step):
        @pl.when(is_source & (step < CHUNKS))
        def _():
            cross(step).wait_recv()
            near[rel, part(step)] = chosen[part(step)] * (1 - from_across) + crossed[part(step)] * from_across
            ring(rel, step, 1, up_s).start()
            ring(rel, step, -1, down_s).start()
            hand(rel, step).start()

        for h in range(1, 6):
            for by in (1, -1):
                t = lax.rem(rel - by * h + planes, planes)
                reach = up_reach(t) if by == 1 else down_reach(t)
                lead = STEPS - 1 if by == 1 else 0
                behind = jnp.where(t == lead, 0, 0 if h == 1 else CHUNKS - LAG)
                k = step - LAG * h - behind

                @pl.when((t < STEPS) & (h <= reach) & (k >= 0) & (k < CHUNKS))
                def _():
                    sems = up_s if by == 1 else down_s
                    ring(t, k, by, sems).wait_recv()

                    @pl.when(h < reach)
                    def _():
                        ring(t, k, by, sems).start()

                    hand(t, k).start()

    for copy in slabs:
        copy.wait_recv()

    @pl.loop(0, STEPS * CHUNKS)
    def _(i):
        hand(i // CHUNKS, lax.rem(i, CHUNKS)).wait_recv()

    @pl.loop(0, row_blocks)
    def _(a):
        for t in range(STEPS):
            for b in range(col_blocks):
                slot = slots[t, a * col_blocks + b]
                lanes = slice((t * col_blocks + b) * BLOCK, (t * col_blocks + b + 1) * BLOCK)
                for source, half in ((near, core), (far, 1 - core)):
                    wide[pl.ds(pl.multiple_of(a * BLOCK + half * HALF, HALF), HALF), lanes] = source[t, slot]

    @pl.loop(0, row_blocks // 2)
    def _(i):
        at = pl.ds(pl.multiple_of(i * 2 * BLOCK, 2 * BLOCK), 2 * BLOCK)
        total = jnp.dot(wide[at, :], r_all[...].reshape(STEPS * width, width), preferred_element_type=jnp.float32)
        out[at, :] = total

    @pl.when(is_source)
    def _():
        swap.wait_send()

        @pl.loop(0, CHUNKS)
        def _(k):
            cross(k).wait_send()

    for copy in slabs:
        copy.wait_send()

    @pl.loop(0, STEPS * CHUNKS)
    def _(i):
        t, k = i // CHUNKS, lax.rem(i, CHUNKS)
        hand(t, k).wait_send()

        @pl.when(lax.rem(rel - t + planes, planes) < up_reach(t))
        def _():
            ring(t, k, 1, up_s).wait_send()

        @pl.when(lax.rem(t - rel + planes, planes) < down_reach(t))
        def _():
            ring(t, k, -1, down_s).wait_send()


def shards(density, block_mask, owner):
    rows, width = density.shape
    n_row, n_col = lax.axis_size("row"), lax.axis_size("col")
    dma = pltpu.SemaphoreType.DMA
    bf16 = jnp.bfloat16
    piece = (CAP, HALF, BLOCK)
    return pl.pallas_call(
        functools.partial(kernel, n_row, n_col),
        out_shape=jax.ShapeDtypeStruct((rows, width), jnp.float32),
        in_specs=[
            pl.BlockSpec(memory_space=pl.ANY),
            pl.BlockSpec(memory_space=pltpu.SMEM),
            pl.BlockSpec(memory_space=pltpu.SMEM),
        ],
        out_specs=pl.BlockSpec(memory_space=pltpu.VMEM),
        scratch_shapes=[
            pltpu.VMEM((width // BLOCK, rows // BLOCK + 1, BLOCK, BLOCK), bf16),
            pltpu.SMEM((4 * rows // BLOCK + 1,), jnp.int32),
            pltpu.SMEM((STEPS, rows // BLOCK * (width // BLOCK)), jnp.int32),
            pltpu.VMEM((3, *piece), bf16),
            pltpu.VMEM(piece, bf16),
            pltpu.VMEM(piece, bf16),
            pltpu.VMEM((STEPS, CAP + 1, HALF, BLOCK), bf16),
            pltpu.VMEM((STEPS, CAP + 1, HALF, BLOCK), bf16),
            pltpu.VMEM((STEPS - 1, width, width), bf16),
            pltpu.VMEM((STEPS, width, width), bf16),
            pltpu.VMEM((rows, STEPS * width), bf16),
            dma((width // BLOCK,)), dma, dma, dma((CHUNKS,)), dma((CHUNKS,)),
            dma((STEPS, CHUNKS)), dma((STEPS, CHUNKS)), dma((STEPS, CHUNKS)),
            dma((STEPS, CHUNKS)), dma((STEPS, CHUNKS)),
            dma((STEPS - 1,)), dma((STEPS - 1,)),
        ],
        compiler_params=pltpu.CompilerParams(
            collective_id=0, has_side_effects=True, vmem_limit_bytes=48 * 1024 * 1024
        ),
        cost_estimate=pl.CostEstimate(
            flops=2 * rows * width * width * STEPS, bytes_accessed=rows * width * 6, transcendentals=0
        ),
        name="fox",
    )(density.reshape(rows // BLOCK, BLOCK, width), block_mask, owner)


def solution(mesh):
    placed = (P("col", "row"), P(), P())
    return jax.shard_map(
        shards, mesh=mesh, in_specs=placed, out_specs=P("col", "row"), check_vma=False
    )
```

time: 321 us -> 57.4 us (0.18)
  the two profiles are of different devices: /device:TPU:9 before, /device:TPU:41 now
where the time goes in v1:
time: 57.4 us; the launch traced here: 57.2 us
  Pallas kernels  53 us (92%)
  local copies, waits for them, and re-layouts  4.16 us (7%)
    pallas_call x1, Pallas kernels, shards(): pl.pallas_call(functools.partial(kernel, n_row, n_col), out_shape=jax.Sha...  53 us
    unnamed x7, local copies, waits for them, and re-layouts  4.16 us

profile of v1, /device:TPU:41, one launch (start us, length us, event | category | flops | bytes accessed | tf_op | source)
XLA Modules:
  0.0 57.2 jit_solution(1649176136922299613)
XLA Ops:
  0.0 0.0 copy-start
  0.0 1.3 %copy-done = bf16[1536,384]{1,0:T(8,128)(2,1)S(1)} copy-done((bf16[1536,384]{1,0:T(8,128)(2,1)S(1)}, bf16[1536,384]{1,0:T(8,128)(2,1)}, u32[]{:S(2)}) %copy-start) | copy-done | bytes 1179672
  1.3 0.0 copy-start.1
  1.3 0.8 %copy-done.1 = s32[96,96]{1,0:T(8,128)S(1)} copy-done((s32[96,96]{1,0:T(8,128)S(1)}, s32[96,96]{1,0:T(8,128)}, u32[]{:S(2)}) %copy-start.1) | copy-done | bytes 36888
  2.1 0.0 copy-start.2
  2.1 0.7 %copy-done.2 = s32[4,8]{1,0:T(4,128)S(1)} copy-done((s32[4,8]{1,0:T(4,128)S(1)}, s32[4,8]{1,0:T(4,128)}, u32[]{:S(2)}) %copy-start.2) | copy-done | bytes 152
  2.8 53.0 %fox.1 = f32[1536,384]{1,0:T(8,128)S(1)} custom-call(bf16[12,128,384]{2,1,0:T(8,128)(2,1)S(1)} %bitcast.1, s32[96,96]{1,0:T(8,128)S(1)} %copy-done.1, s32[4,8]{1,0:T(4,128)S(1)} %copy-done.2), custom_call_target="tpu_custom_call" | custom-call | flops 1811939328 | bytes 3538944 | tf_op jit(solution)/shard_map/fox/pallas_call | solution.py:238
  55.8 1.4 %copy.5 = f32[1536,384]{1,0:T(8,128)} copy(f32[1536,384]{1,0:T(8,128)S(1)} %fox.1) | data formatting | bytes 4718592
Async XLA Ops:
  0.0 1.3 %copy-start = (bf16[1536,384]{1,0:T(8,128)(2,1)S(1)}, bf16[1536,384]{1,0:T(8,128)(2,1)}, u32[]{:S(2)}) copy-start(bf16[1536,384]{1,0:T(8,128)(2,1)} %param.3) | copy-start | bytes 3538948
  1.3 0.8 %copy-start.1 = (s32[96,96]{1,0:T(8,128)S(1)}, s32[96,96]{1,0:T(8,128)}, u32[]{:S(2)}) copy-start(s32[96,96]{1,0:T(8,128)} %mask.1) | copy-start | bytes 110596
  2.1 0.7 %copy-start.2 = (s32[4,8]{1,0:T(4,128)S(1)}, s32[4,8]{1,0:T(4,128)}, u32[]{:S(2)}) copy-start(s32[4,8]{1,0:T(4,128)} %owner.1) | copy-start | bytes 388

commit v2 on v1

v2 whole, which is shorter than its diff:
```python
import functools

import jax
import jax.numpy as jnp
from jax import lax
from jax.experimental import pallas as pl
from jax.experimental.pallas import tpu as pltpu
from jax.sharding import PartitionSpec as P

BLOCK = 128
STEPS = 4
CAP = 21
HALF = BLOCK // 2
CHUNKS = 7
SPAN = CAP // CHUNKS
LAG = 4
SHIFT = 3
DETOUR = 12
READY = 14
UNITS = 6
UP = (3, 3, 4, 4)
MESH = pl.DeviceIdType.MESH


def kernel(
    n_row, n_col, density, mask_in, owner_in, out,
    mask, owner, tile, nxt, slots, packed, swapped, chosen, crossed, held_0, held_1, held_2, held_3, r_send, r_all, passing,
    load_sem, table_sem, swap_s, swap_r, cross_s, cross_r, up_s, down_s, ring_r, mate_s, mate_r, slab_s, slab_r, pass_s, pass_r,
):
    held = (held_0, held_1, held_2, held_3)
    g = lax.axis_index("col")
    j = lax.axis_index("row")
    sub = n_row // n_col
    planes = n_col
    plane = j // sub
    place = lax.rem(j, sub)
    core = lax.rem(place, 2)
    rel = lax.rem(plane - g + planes, planes)
    is_source = rel < STEPS
    row_blocks, _, width = density.shape
    col_blocks = width // BLOCK
    my_rows = pl.ds(pl.multiple_of(core * HALF, HALF), HALF)
    mate_rows = pl.ds(pl.multiple_of((1 - core) * HALF, HALF), HALF)

    def at_plane(by):
        return {"col": g, "row": lax.rem(plane + by + planes, planes) * sub + place}

    def at_grid_row(by):
        return {"col": lax.rem(g + by + n_col, n_col), "row": j}

    mate = {"col": g, "row": plane * sub + place + 1 - 2 * core}
    across = {"col": g, "row": plane * sub + lax.rem(place + 2, sub)}

    barrier = pltpu.get_barrier_semaphore()
    odd = lax.rem(g, 2)
    senders = [mate, across, at_plane(1), at_plane(-1), at_grid_row(1), at_grid_row(2)]
    senders += [at_grid_row(STEPS - 1 - 2 * (STEPS - 1) * odd)]
    for device in senders:
        pl.semaphore_signal(barrier, inc=1, device_id=device, device_id_type=MESH)

    tables = [
        pltpu.make_async_copy(mask_in, mask, table_sem.at[0]),
        pltpu.make_async_copy(owner_in, owner, table_sem.at[1]),
    ]
    loads = [
        pltpu.make_async_copy(
            density.at[:, :, pl.ds(b * BLOCK, BLOCK)], tile.at[b, pl.ds(0, row_blocks)], load_sem.at[b]
        )
        for b in range(col_blocks)
    ]
    for copy in tables + loads:
        copy.start()
    zero = jnp.zeros((BLOCK, BLOCK), jnp.bfloat16)
    for b in range(col_blocks):
        tile[b, row_blocks] = zero
    for t in range(STEPS):
        held[t][CAP] = zero
    for copy in tables:
        copy.wait()

    first = jnp.int32(4 * (row_blocks - 1))
    nxt[4 * row_blocks] = first
    for q in reversed(range(4 * row_blocks)):
        a, b = q // 4, q % 4
        if b < col_blocks:
            bit = mask[g * row_blocks + a, j * col_blocks + b]
            first = first + bit * (q - first)
        nxt[q] = first

    for load in loads:
        load.wait()

    q = nxt[0]
    for s in range(CAP):
        packed[s] = tile[q & 3, q >> 2]
        q = nxt[q + 1]

    @pl.when(odd == 0)
    def _():
        pl.semaphore_signal(barrier, inc=1, device_id=at_grid_row(-2), device_id_type=MESH)

    pl.semaphore_wait(barrier, len(senders) + 1 - odd)

    def remote(src, dst, send, recv, device):
        return pltpu.make_async_remote_copy(
            src_ref=src, dst_ref=dst, send_sem=send, recv_sem=recv, device_id=device, device_id_type=MESH
        )

    def part(k):
        return pl.ds(k * SPAN, SPAN)

    swap = remote(packed.at[:, mate_rows], swapped.at[:], swap_s, swap_r, mate)

    def cross(k):
        return remote(chosen.at[part(k)], crossed.at[part(k)], cross_s.at[k], cross_r.at[k], across)

    def ring(t, k, by, sems):
        span = held[t].at[part(k), my_rows]
        return remote(span, span, sems.at[t, k], ring_r.at[t, k], at_plane(by))

    early = CHUNKS // 2 + 1

    def hand(t, late):
        blocks = pl.ds(early * SPAN, (CHUNKS - early) * SPAN) if late else pl.ds(0, early * SPAN)
        span = held[t].at[blocks, my_rows]
        return remote(span, span, mate_s.at[t, late], mate_r.at[t, late], mate)

    slabs = [
        remote(r_send.at[t - 1], r_all.at[t], slab_s.at[t - 1], slab_r.at[t - 1], at_grid_row(-t))
        for t in range(1, STEPS)
    ]
    detours = lax.rem(g, 2) == 0
    detour = remote(r_send.at[STEPS - 2], passing.at[:], pass_s.at[0], pass_r, at_grid_row(2))
    onto = remote(passing.at[:], r_all.at[STEPS - 1], pass_s.at[1], slab_r.at[STEPS - 2], at_grid_row(STEPS - 1))

    @pl.when(is_source)
    def _():
        swap.start()

    pick = owner[jnp.minimum(rel, STEPS - 1), g] & (sub - 1)

    for t in range(STEPS):
        slab = (owner[t, lax.rem(g - t + n_col, n_col)] & (sub - 1)) * col_blocks
        for a in range(col_blocks):
            for b in range(col_blocks):
                bit = mask[g * row_blocks + slab + a, j * col_blocks + b]
                block = tile[b, row_blocks + bit * (slab + a - row_blocks)]
                if t == 0:
                    r_all[0, a * BLOCK : (a + 1) * BLOCK, b * BLOCK : (b + 1) * BLOCK] = block
                else:
                    r_send[t - 1, a * BLOCK : (a + 1) * BLOCK, b * BLOCK : (b + 1) * BLOCK] = block

    mine = 1 - ((pick + core) & 1)

    def whole(flag):
        return jnp.full((SPAN, HALF, BLOCK), flag, jnp.int32).astype(jnp.float32).astype(jnp.bfloat16)

    @pl.when(is_source)
    def _():
        swap.wait_recv()
        own = whole(mine)

        @pl.loop(0, CHUNKS)
        def _(k):
            chosen[part(k)] = packed[part(k), my_rows] * own + swapped[part(k)] * (1 - own)
            cross(k).start()

    slabs[1].start()
    slabs[0].start()

    @pl.when(detours)
    def _():
        detour.start()

    @pl.when(jnp.logical_not(detours))
    def _():
        slabs[2].start()


    for t in range(STEPS):
        at = owner[t, g] * col_blocks
        count = jnp.int32(0)
        for a in range(row_blocks):
            for b in range(col_blocks):
                bit = mask[g * row_blocks + a, at + b]
                slots[t, a * col_blocks + b] = CAP + bit * (count - CAP)
                count = count + bit
    out[...] = jnp.zeros_like(out)

    moved = whole(((pick >> 1) + place // 2) & 1)

    route = []
    for t in range(STEPS):
        above = lax.rem(rel - t + planes, planes)
        up = above <= UP[t]
        hops = jnp.where(up, above, planes - above)
        nearer = jnp.maximum(jnp.minimum(jnp.where(up, STEPS - 1 - t, t), hops - 1), 0)
        onward = (hops > 0) & (hops < jnp.where(up, UP[t], planes - 1 - UP[t]))
        route.append((up, onward, LAG * hops + SHIFT * nearer))

    unit_rows = row_blocks // UNITS

    @pl.loop(0, LAG * max(UP) + SHIFT * (STEPS - 1) + CHUNKS + 1 + UNITS)
    def _(step):
        @pl.when(is_source & (step < CHUNKS))
        def _():
            cross(step).wait_recv()

        for t in range(STEPS):
            up, onward, begin = route[t]
            k = step - begin

            @pl.when((k >= 0) & (k < CHUNKS))
            def _():
                @pl.when(rel == t)
                def _():
                    held[t][part(k), my_rows] = chosen[part(k)] * (1 - moved) + crossed[part(k)] * moved
                    ring(t, k, 1, up_s).start()
                    ring(t, k, -1, down_s).start()

                @pl.when(rel != t)
                def _():
                    ring(t, k, 1, up_s).wait_recv()

                @pl.when(onward & up)
                def _():
                    ring(t, k, 1, up_s).start()

                @pl.when(onward & jnp.logical_not(up))
                def _():
                    ring(t, k, -1, down_s).start()

                @pl.when(k == early - 1)
                def _():
                    hand(t, 0).start()

                @pl.when(k == CHUNKS - 1)
                def _():
                    hand(t, 1).start()

        @pl.when(detours & (step == DETOUR))
        def _():
            detour.wait_recv()
            onto.start()

        for t in range(STEPS):
            unit = step - jnp.maximum(route[t][2] + CHUNKS + 1, READY + t)

            @pl.when((unit >= 0) & (unit < UNITS))
            def _():
                @pl.when(unit == 0)
                def _():
                    hand(t, 0).wait_recv()
                    hand(t, 1).wait_recv()
                    if t > 0:
                        slabs[t - 1].wait_recv()

                lines = [
                    jnp.concatenate(
                        [
                            held[t][slots[t, (unit * unit_rows + a) * col_blocks + b]]
                            for b in range(col_blocks)
                        ],
                        axis=1,
                    )
                    for a in range(unit_rows)
                ]
                at = pl.ds(pl.multiple_of(unit * unit_rows * BLOCK, unit_rows * BLOCK), unit_rows * BLOCK)
                out[at, :] += jnp.dot(
                    jnp.concatenate(lines, axis=0), r_all[t], preferred_element_type=jnp.float32
                )

    @pl.when(is_source)
    def _():
        swap.wait_send()

        @pl.loop(0, CHUNKS)
        def _(k):
            cross(k).wait_send()

    slabs[0].wait_send()
    slabs[1].wait_send()

    @pl.when(detours)
    def _():
        detour.wait_send()
        onto.wait_send()

    @pl.when(jnp.logical_not(detours))
    def _():
        slabs[2].wait_send()

    for t in range(STEPS):
        up, onward, _ = route[t]
        hand(t, 0).wait_send()
        hand(t, 1).wait_send()

        @pl.when((rel == t) | (onward & up))
        def _():
            @pl.loop(0, CHUNKS)
            def _(k):
                ring(t, k, 1, up_s).wait_send()

        @pl.when((rel == t) | (onward & jnp.logical_not(up)))
        def _():
            @pl.loop(0, CHUNKS)
            def _(k):
                ring(t, k, -1, down_s).wait_send()


def shards(density, block_mask, owner):
    rows, width = density.shape
    row_blocks, col_blocks = rows // BLOCK, width // BLOCK
    n_row, n_col = lax.axis_size("row"), lax.axis_size("col")
    dma = pltpu.SemaphoreType.DMA
    bf16 = jnp.bfloat16
    piece = (CAP, HALF, BLOCK)
    return pl.pallas_call(
        functools.partial(kernel, n_row, n_col),
        out_shape=jax.ShapeDtypeStruct((rows, width), jnp.float32),
        in_specs=[pl.BlockSpec(memory_space=pltpu.HBM)] * 3,
        out_specs=pl.BlockSpec(memory_space=pltpu.VMEM),
        scratch_shapes=[
            pltpu.SMEM(block_mask.shape, jnp.int32),
            pltpu.SMEM(owner.shape, jnp.int32),
            pltpu.VMEM((col_blocks, row_blocks + 1, BLOCK, BLOCK), bf16),
            pltpu.SMEM((4 * row_blocks + 1,), jnp.int32),
            pltpu.SMEM((STEPS, row_blocks * col_blocks), jnp.int32),
            pltpu.VMEM((CAP, BLOCK, BLOCK), bf16),
            pltpu.VMEM(piece, bf16),
            pltpu.VMEM(piece, bf16),
            pltpu.VMEM(piece, bf16),
            *[pltpu.VMEM((CAP + 1, BLOCK, BLOCK), bf16)] * STEPS,
            pltpu.VMEM((STEPS - 1, width, width), bf16),
            pltpu.VMEM((STEPS, width, width), bf16),
            pltpu.VMEM((width, width), bf16),
            dma((col_blocks,)), dma((2,)), dma, dma, dma((CHUNKS,)), dma((CHUNKS,)),
            dma((STEPS, CHUNKS)), dma((STEPS, CHUNKS)), dma((STEPS, CHUNKS)),
            dma((STEPS, 2)), dma((STEPS, 2)),
            dma((STEPS - 1,)), dma((STEPS - 1,)), dma((2,)), dma,
        ],
        compiler_params=pltpu.CompilerParams(
            collective_id=0, has_side_effects=True, vmem_limit_bytes=48 * 1024 * 1024
        ),
        cost_estimate=pl.CostEstimate(
            flops=2 * rows * width * width * STEPS, bytes_accessed=rows * width * 6, transcendentals=0
        ),
        name="fox",
    )(density.reshape(row_blocks, BLOCK, width), block_mask, owner)


def solution(mesh):
    placed = (P("col", "row"), P(), P())
    return jax.shard_map(
        shards, mesh=mesh, in_specs=placed, out_specs=P("col", "row"), check_vma=False
    )
```

time: 57.4 us -> 50.8 us (0.89)
  the two profiles are of different devices: /device:TPU:41 before, /device:TPU:9 now
where the time goes in v2:
time: 50.8 us; the launch traced here: 50.6 us
  Pallas kernels  46.4 us (91%)
  local copies, waits for them, and re-layouts  4.16 us (8%)
    pallas_call x1, Pallas kernels, shards(): pl.pallas_call(functools.partial(kernel, n_row, n_col), out_shape=jax.Sha...  46.4 us
    unnamed x7, local copies, waits for them, and re-layouts  4.16 us

profile of v2, /device:TPU:9, one launch (start us, length us, event | category | flops | bytes accessed | tf_op | source)
XLA Modules:
  0.0 50.6 jit_solution(8129495816993925170)
XLA Ops:
  0.0 0.0 copy-start
  0.0 1.3 %copy-done = bf16[1536,384]{1,0:T(8,128)(2,1)S(1)} copy-done((bf16[1536,384]{1,0:T(8,128)(2,1)S(1)}, bf16[1536,384]{1,0:T(8,128)(2,1)}, u32[]{:S(2)}) %copy-start) | copy-done | bytes 1179672
  1.3 0.0 copy-start.1
  1.3 0.8 %copy-done.1 = s32[96,96]{1,0:T(8,128)S(1)} copy-done((s32[96,96]{1,0:T(8,128)S(1)}, s32[96,96]{1,0:T(8,128)}, u32[]{:S(2)}) %copy-start.1) | copy-done | bytes 36888
  2.1 0.0 copy-start.2
  2.1 0.7 %copy-done.2 = s32[4,8]{1,0:T(4,128)S(1)} copy-done((s32[4,8]{1,0:T(4,128)S(1)}, s32[4,8]{1,0:T(4,128)}, u32[]{:S(2)}) %copy-start.2) | copy-done | bytes 152
  2.8 46.4 %fox.1 = f32[1536,384]{1,0:T(8,128)S(1)} custom-call(bf16[12,128,384]{2,1,0:T(8,128)(2,1)S(1)} %bitcast.1, s32[96,96]{1,0:T(8,128)S(1)} %copy-done.1, s32[4,8]{1,0:T(4,128)S(1)} %copy-done.2), custom_call_target="tpu_custom_call" | custom-call | flops 1811939328 | bytes 3538944 | tf_op jit(solution)/shard_map/fox/pallas_call | solution.py:318
  49.2 1.4 %copy.5 = f32[1536,384]{1,0:T(8,128)} copy(f32[1536,384]{1,0:T(8,128)S(1)} %fox.1) | data formatting | bytes 4718592
Async XLA Ops:
  0.0 1.3 %copy-start = (bf16[1536,384]{1,0:T(8,128)(2,1)S(1)}, bf16[1536,384]{1,0:T(8,128)(2,1)}, u32[]{:S(2)}) copy-start(bf16[1536,384]{1,0:T(8,128)(2,1)} %param.3) | copy-start | bytes 3538948
  1.3 0.8 %copy-start.1 = (s32[96,96]{1,0:T(8,128)S(1)}, s32[96,96]{1,0:T(8,128)}, u32[]{:S(2)}) copy-start(s32[96,96]{1,0:T(8,128)} %mask_in.1) | copy-start | bytes 110596
  2.1 0.7 %copy-start.2 = (s32[4,8]{1,0:T(4,128)S(1)}, s32[4,8]{1,0:T(4,128)}, u32[]{:S(2)}) copy-start(s32[4,8]{1,0:T(4,128)} %owner_in.1) | copy-start | bytes 388

commit v3 on v2

--- a/solution.py
+++ b/solution.py
@@ -15,9 +15,10 @@
 SPAN = CAP // CHUNKS
 LAG = 4
 SHIFT = 3
+AFTER = 2
 DETOUR = 12
-READY = 14
-UNITS = 6
+READY = 16
+UNITS = 4
 UP = (3, 3, 4, 4)
 MESH = pl.DeviceIdType.MESH
 
@@ -196,11 +197,11 @@
         hops = jnp.where(up, above, planes - above)
         nearer = jnp.maximum(jnp.minimum(jnp.where(up, STEPS - 1 - t, t), hops - 1), 0)
         onward = (hops > 0) & (hops < jnp.where(up, UP[t], planes - 1 - UP[t]))
-        route.append((up, onward, LAG * hops + SHIFT * nearer))
+        route.append((up, onward, jnp.where(hops > 0, LAG * hops + SHIFT * nearer + AFTER, 0)))
 
     unit_rows = row_blocks // UNITS
 
-    @pl.loop(0, LAG * max(UP) + SHIFT * (STEPS - 1) + CHUNKS + 1 + UNITS)
+    @pl.loop(0, LAG * max(UP) + SHIFT * (STEPS - 1) + AFTER + CHUNKS + 1 + UNITS)
     def _(step):
         @pl.when(is_source & (step < CHUNKS))
         def _():

time: 50.8 us -> 48.2 us (0.949)
  Pallas kernels: 46.4 us -> 43.8 us
    pallas_call x1, Pallas kernels: 46.4 us -> 43.8 us  [shards(): pl.pallas_call(functools.partial(kernel, n_row, n_col), out_shape=jax.Sha...]
where the time goes in v3:
time: 48.2 us; the launch traced here: 48 us
  Pallas kernels  43.8 us (91%)
  local copies, waits for them, and re-layouts  4.16 us (9%)
    pallas_call x1, Pallas kernels, shards(): pl.pallas_call(functools.partial(kernel, n_row, n_col), out_shape=jax.Sha...  43.8 us
    unnamed x7, local copies, waits for them, and re-layouts  4.16 us

profile of v3, /device:TPU:9, one launch (start us, length us, event | category | flops | bytes accessed | tf_op | source)
XLA Modules:
  0.0 48.0 jit_solution(8250420980745496045)
XLA Ops:
  0.0 0.0 copy-start
  0.0 1.3 %copy-done = bf16[1536,384]{1,0:T(8,128)(2,1)S(1)} copy-done((bf16[1536,384]{1,0:T(8,128)(2,1)S(1)}, bf16[1536,384]{1,0:T(8,128)(2,1)}, u32[]{:S(2)}) %copy-start) | copy-done | bytes 1179672
  1.3 0.0 copy-start.1
  1.3 0.8 %copy-done.1 = s32[96,96]{1,0:T(8,128)S(1)} copy-done((s32[96,96]{1,0:T(8,128)S(1)}, s32[96,96]{1,0:T(8,128)}, u32[]{:S(2)}) %copy-start.1) | copy-done | bytes 36888
  2.1 0.0 copy-start.2
  2.1 0.7 %copy-done.2 = s32[4,8]{1,0:T(4,128)S(1)} copy-done((s32[4,8]{1,0:T(4,128)S(1)}, s32[4,8]{1,0:T(4,128)}, u32[]{:S(2)}) %copy-start.2) | copy-done | bytes 152
  2.8 43.8 %fox.1 = f32[1536,384]{1,0:T(8,128)S(1)} custom-call(bf16[12,128,384]{2,1,0:T(8,128)(2,1)S(1)} %bitcast.1, s32[96,96]{1,0:T(8,128)S(1)} %copy-done.1, s32[4,8]{1,0:T(4,128)S(1)} %copy-done.2), custom_call_target="tpu_custom_call" | custom-call | flops 1811939328 | bytes 3538944 | tf_op jit(solution)/shard_map/fox/pallas_call | solution.py:319
  46.6 1.4 %copy.5 = f32[1536,384]{1,0:T(8,128)} copy(f32[1536,384]{1,0:T(8,128)S(1)} %fox.1) | data formatting | bytes 4718592
Async XLA Ops:
  0.0 1.3 %copy-start = (bf16[1536,384]{1,0:T(8,128)(2,1)S(1)}, bf16[1536,384]{1,0:T(8,128)(2,1)}, u32[]{:S(2)}) copy-start(bf16[1536,384]{1,0:T(8,128)(2,1)} %param.3) | copy-start | bytes 3538948
  1.3 0.8 %copy-start.1 = (s32[96,96]{1,0:T(8,128)S(1)}, s32[96,96]{1,0:T(8,128)}, u32[]{:S(2)}) copy-start(s32[96,96]{1,0:T(8,128)} %mask_in.1) | copy-start | bytes 110596
  2.1 0.7 %copy-start.2 = (s32[4,8]{1,0:T(4,128)S(1)}, s32[4,8]{1,0:T(4,128)}, u32[]{:S(2)}) copy-start(s32[4,8]{1,0:T(4,128)} %owner_in.1) | copy-start | bytes 388

commit v4 on v3

--- a/solution.py
+++ b/solution.py
@@ -17,18 +17,18 @@
 SHIFT = 3
 AFTER = 2
 DETOUR = 12
-READY = 16
+READY = 17
 UNITS = 4
 UP = (3, 3, 4, 4)
 MESH = pl.DeviceIdType.MESH
 
 
 def kernel(
-    n_row, n_col, density, mask_in, owner_in, out,
-    mask, owner, tile, nxt, slots, packed, swapped, chosen, crossed, held_0, held_1, held_2, held_3, r_send, r_all, passing,
-    load_sem, table_sem, swap_s, swap_r, cross_s, cross_r, up_s, down_s, ring_r, mate_s, mate_r, slab_s, slab_r, pass_s, pass_r,
+    n_row, n_col, density, table_in, result,
+    table, tile, nxt, slots, packed, swapped, chosen, crossed, near_0, near_1, near_2, near_3, far_0, far_1, far_2, far_3, r_send, r_all, passing, out,
+    load_sem, table_sem, swap_s, swap_r, cross_s, cross_r, up_s, down_s, ring_r, mate_s, mate_r, slab_s, slab_r, pass_s, pass_r, out_sem,
 ):
-    held = (held_0, held_1, held_2, held_3)
+    near, far = (near_0, near_1, near_2, near_3), (far_0, far_1, far_2, far_3)
     g = lax.axis_index("col")
     j = lax.axis_index("row")
     sub = n_row // n_col
@@ -39,6 +39,7 @@
     rel = lax.rem(plane - g + planes, planes)
     is_source = rel < STEPS
     row_blocks, _, width = density.shape
+    len_mask = n_col * row_blocks
     col_blocks = width // BLOCK
     my_rows = pl.ds(pl.multiple_of(core * HALF, HALF), HALF)
     mate_rows = pl.ds(pl.multiple_of((1 - core) * HALF, HALF), HALF)
@@ -59,10 +60,7 @@
     for device in senders:
         pl.semaphore_signal(barrier, inc=1, device_id=device, device_id_type=MESH)
 
-    tables = [
-        pltpu.make_async_copy(mask_in, mask, table_sem.at[0]),
-        pltpu.make_async_copy(owner_in, owner, table_sem.at[1]),
-    ]
+    tables = [pltpu.make_async_copy(table_in, table, table_sem.at[0])]
     loads = [
         pltpu.make_async_copy(
             density.at[:, :, pl.ds(b * BLOCK, BLOCK)], tile.at[b, pl.ds(0, row_blocks)], load_sem.at[b]
@@ -75,7 +73,8 @@
     for b in range(col_blocks):
         tile[b, row_blocks] = zero
     for t in range(STEPS):
-        held[t][CAP] = zero
+        near[t][CAP] = zero[:HALF]
+        far[t][CAP] = zero[:HALF]
     for copy in tables:
         copy.wait()
 
@@ -84,7 +83,7 @@
     for q in reversed(range(4 * row_blocks)):
         a, b = q // 4, q % 4
         if b < col_blocks:
-            bit = mask[g * row_blocks + a, j * col_blocks + b]
+            bit = table[g * row_blocks + a, j * col_blocks + b]
             first = first + bit * (q - first)
         nxt[q] = first
 
@@ -92,7 +91,7 @@
         load.wait()
 
     q = nxt[0]
-    for s in range(CAP):
+    for s in range(SPAN):
         packed[s] = tile[q & 3, q >> 2]
         q = nxt[q + 1]
 
@@ -110,21 +109,22 @@
     def part(k):
         return pl.ds(k * SPAN, SPAN)
 
-    swap = remote(packed.at[:, mate_rows], swapped.at[:], swap_s, swap_r, mate)
+    def swap(n):
+        blocks = pl.ds(0, SPAN) if n == 0 else pl.ds(SPAN, CAP - SPAN)
+        return remote(packed.at[blocks, mate_rows], swapped.at[blocks], swap_s.at[n], swap_r.at[n], mate)
 
     def cross(k):
         return remote(chosen.at[part(k)], crossed.at[part(k)], cross_s.at[k], cross_r.at[k], across)
 
     def ring(t, k, by, sems):
-        span = held[t].at[part(k), my_rows]
+        span = near[t].at[part(k)]
         return remote(span, span, sems.at[t, k], ring_r.at[t, k], at_plane(by))
 
-    early = CHUNKS // 2 + 1
+    early = CHUNKS - 2
 
     def hand(t, late):
         blocks = pl.ds(early * SPAN, (CHUNKS - early) * SPAN) if late else pl.ds(0, early * SPAN)
-        span = held[t].at[blocks, my_rows]
-        return remote(span, span, mate_s.at[t, late], mate_r.at[t, late], mate)
+        return remote(near[t].at[blocks], far[t].at[blocks], mate_s.at[t, late], mate_r.at[t, late], mate)
 
     slabs = [
         remote(r_send.at[t - 1], r_all.at[t], slab_s.at[t - 1], slab_r.at[t - 1], at_grid_row(-t))
@@ -136,15 +136,23 @@
 
     @pl.when(is_source)
     def _():
-        swap.start()
-
-    pick = owner[jnp.minimum(rel, STEPS - 1), g] & (sub - 1)
-
-    for t in range(STEPS):
-        slab = (owner[t, lax.rem(g - t + n_col, n_col)] & (sub - 1)) * col_blocks
+        swap(0).start()
+
+    for s in range(SPAN, CAP):
+        packed[s] = tile[q & 3, q >> 2]
+        q = nxt[q + 1]
+
+    @pl.when(is_source)
+    def _():
+        swap(1).start()
+
+    pick = table[len_mask + jnp.minimum(rel, STEPS - 1), g] & (sub - 1)
+
+    for t in range(STEPS):
+        slab = (table[len_mask + t, lax.rem(g - t + n_col, n_col)] & (sub - 1)) * col_blocks
         for a in range(col_blocks):
             for b in range(col_blocks):
-                bit = mask[g * row_blocks + slab + a, j * col_blocks + b]
+                bit = table[g * row_blocks + slab + a, j * col_blocks + b]
                 block = tile[b, row_blocks + bit * (slab + a - row_blocks)]
                 if t == 0:
                     r_all[0, a * BLOCK : (a + 1) * BLOCK, b * BLOCK : (b + 1) * BLOCK] = block
@@ -158,11 +166,15 @@
 
     @pl.when(is_source)
     def _():
-        swap.wait_recv()
+        swap(0).wait_recv()
         own = whole(mine)
 
         @pl.loop(0, CHUNKS)
         def _(k):
+            @pl.when(k == 1)
+            def _():
+                swap(1).wait_recv()
+
             chosen[part(k)] = packed[part(k), my_rows] * own + swapped[part(k)] * (1 - own)
             cross(k).start()
 
@@ -179,11 +191,11 @@
 
 
     for t in range(STEPS):
-        at = owner[t, g] * col_blocks
+        at = table[len_mask + t, g] * col_blocks
         count = jnp.int32(0)
         for a in range(row_blocks):
             for b in range(col_blocks):
-                bit = mask[g * row_blocks + a, at + b]
+                bit = table[g * row_blocks + a, at + b]
                 slots[t, a * col_blocks + b] = CAP + bit * (count - CAP)
                 count = count + bit
     out[...] = jnp.zeros_like(out)
@@ -199,7 +211,20 @@
         onward = (hops > 0) & (hops < jnp.where(up, UP[t], planes - 1 - UP[t]))
         route.append((up, onward, jnp.where(hops > 0, LAG * hops + SHIFT * nearer + AFTER, 0)))
 
-    unit_rows = row_blocks // UNITS
+    unit_rows = 2 * row_blocks // UNITS
+    starts = [jnp.maximum(begin + CHUNKS, READY + t) for t, (_, _, begin) in enumerate(route)]
+    ends = functools.reduce(jnp.maximum, [2 * STEPS * start + t for t, start in enumerate(starts)])
+
+    def place_of(unit):
+        half = lax.rem(core + unit // (UNITS // 2), 2)
+        first_row = lax.rem(unit, UNITS // 2) * unit_rows
+        return first_row, pl.ds(pl.multiple_of(half * HALF, HALF), HALF)
+
+    def finished(unit):
+        first_row, lines = place_of(unit)
+        at = pl.ds(first_row, unit_rows)
+        return pltpu.make_async_copy(out.at[at, lines], result.at[at, lines], out_sem.at[unit])
+
 
     @pl.loop(0, LAG * max(UP) + SHIFT * (STEPS - 1) + AFTER + CHUNKS + 1 + UNITS)
     def _(step):
@@ -215,7 +240,7 @@
             def _():
                 @pl.when(rel == t)
                 def _():
-                    held[t][part(k), my_rows] = chosen[part(k)] * (1 - moved) + crossed[part(k)] * moved
+                    near[t][part(k)] = chosen[part(k)] * (1 - moved) + crossed[part(k)] * moved
                     ring(t, k, 1, up_s).start()
                     ring(t, k, -1, down_s).start()
 
@@ -245,39 +270,52 @@
             onto.start()
 
         for t in range(STEPS):
-            unit = step - jnp.maximum(route[t][2] + CHUNKS + 1, READY + t)
+            unit = step - starts[t]
 
             @pl.when((unit >= 0) & (unit < UNITS))
             def _():
                 @pl.when(unit == 0)
                 def _():
+                    if t > 0:
+                        slabs[t - 1].wait_recv()
+
+                @pl.when(unit == UNITS // 2)
+                def _():
                     hand(t, 0).wait_recv()
                     hand(t, 1).wait_recv()
-                    if t > 0:
-                        slabs[t - 1].wait_recv()
-
-                lines = [
-                    jnp.concatenate(
-                        [
-                            held[t][slots[t, (unit * unit_rows + a) * col_blocks + b]]
-                            for b in range(col_blocks)
-                        ],
-                        axis=1,
-                    )
-                    for a in range(unit_rows)
-                ]
-                at = pl.ds(pl.multiple_of(unit * unit_rows * BLOCK, unit_rows * BLOCK), unit_rows * BLOCK)
-                out[at, :] += jnp.dot(
-                    jnp.concatenate(lines, axis=0), r_all[t], preferred_element_type=jnp.float32
-                )
+
+                first_row, lines = place_of(unit)
+                for rows_of, chosen_half in ((near[t], unit < UNITS // 2), (far[t], unit >= UNITS // 2)):
+
+                    @pl.when(chosen_half)
+                    def _():
+                        left = [
+                            jnp.concatenate(
+                                [rows_of[slots[t, (first_row + a) * col_blocks + b]] for b in range(col_blocks)],
+                                axis=1,
+                            )
+                            for a in range(unit_rows)
+                        ]
+                        product = jnp.dot(
+                            jnp.concatenate(left, axis=0), r_all[t], preferred_element_type=jnp.float32
+                        )
+                        out[pl.ds(first_row, unit_rows), lines] += product.reshape(unit_rows, HALF, width)
+
+                @pl.when(ends == 2 * STEPS * starts[t] + t)
+                def _():
+                    finished(unit).start()
 
     @pl.when(is_source)
     def _():
-        swap.wait_send()
+        swap(0).wait_send()
+        swap(1).wait_send()
 
         @pl.loop(0, CHUNKS)
         def _(k):
             cross(k).wait_send()
+
+    for unit in range(UNITS):
+        finished(unit).wait()
 
     slabs[0].wait_send()
     slabs[1].wait_send()
@@ -316,14 +354,15 @@
     dma = pltpu.SemaphoreType.DMA
     bf16 = jnp.bfloat16
     piece = (CAP, HALF, BLOCK)
+    wide_owner = jnp.pad(owner, ((0, 8 - owner.shape[0]), (0, block_mask.shape[1] - owner.shape[1])))
+    table = jnp.concatenate([block_mask, wide_owner], axis=0)
     return pl.pallas_call(
         functools.partial(kernel, n_row, n_col),
-        out_shape=jax.ShapeDtypeStruct((rows, width), jnp.float32),
-        in_specs=[pl.BlockSpec(memory_space=pltpu.HBM)] * 3,
-        out_specs=pl.BlockSpec(memory_space=pltpu.VMEM),
+        out_shape=jax.ShapeDtypeStruct((row_blocks, BLOCK, width), jnp.float32),
+        in_specs=[pl.BlockSpec(memory_space=pltpu.HBM)] * 2,
+        out_specs=pl.BlockSpec(memory_space=pl.ANY),
         scratch_shapes=[
-            pltpu.SMEM(block_mask.shape, jnp.int32),
-            pltpu.SMEM(owner.shape, jnp.int32),
+            pltpu.SMEM(table.shape, jnp.int32),
             pltpu.VMEM((col_blocks, row_blocks + 1, BLOCK, BLOCK), bf16),
             pltpu.SMEM((4 * row_blocks + 1,), jnp.int32),
             pltpu.SMEM((STEPS, row_blocks * col_blocks), jnp.int32),
@@ -331,14 +370,15 @@
             pltpu.VMEM(piece, bf16),
             pltpu.VMEM(piece, bf16),
             pltpu.VMEM(piece, bf16),
-            *[pltpu.VMEM((CAP + 1, BLOCK, BLOCK), bf16)] * STEPS,
+            *[pltpu.VMEM((CAP + 1, HALF, BLOCK), bf16)] * (2 * STEPS),
             pltpu.VMEM((STEPS - 1, width, width), bf16),
             pltpu.VMEM((STEPS, width, width), bf16),
             pltpu.VMEM((width, width), bf16),
-            dma((col_blocks,)), dma((2,)), dma, dma, dma((CHUNKS,)), dma((CHUNKS,)),
+            pltpu.VMEM((row_blocks, BLOCK, width), jnp.float32),
+            dma((col_blocks,)), dma((2,)), dma((2,)), dma((2,)), dma((CHUNKS,)), dma((CHUNKS,)),
             dma((STEPS, CHUNKS)), dma((STEPS, CHUNKS)), dma((STEPS, CHUNKS)),
             dma((STEPS, 2)), dma((STEPS, 2)),
-            dma((STEPS - 1,)), dma((STEPS - 1,)), dma((2,)), dma,
+            dma((STEPS - 1,)), dma((STEPS - 1,)), dma((2,)), dma, dma((UNITS,)),
         ],
         compiler_params=pltpu.CompilerParams(
             collective_id=0, has_side_effects=True, vmem_limit_bytes=48 * 1024 * 1024
@@ -347,7 +387,7 @@
             flops=2 * rows * width * width * STEPS, bytes_accessed=rows * width * 6, transcendentals=0
         ),
         name="fox",
-    )(density.reshape(row_blocks, BLOCK, width), block_mask, owner)
+    )(density.reshape(row_blocks, BLOCK, width), table).reshape(rows, width)
 
 
 def solution(mesh):

time: 48.2 us -> 47 us (0.975)
  local copies, waits for them, and re-layouts: 4.16 us -> 2.68 us
  Pallas kernels: 43.8 us -> 42.8 us
  other arithmetic: 0 us -> 0.82 us
    unnamed x7 -> x3, local copies, waits for them, and re-layouts: 4.16 us -> 2.68 us
    pallas_call x1, Pallas kernels: 43.8 us -> 42.8 us  [shards(): pl.pallas_call(functools.partial(kernel, n_row, n_col), out_shape=jax.Sha...]
    concatenate x0 -> x1, other arithmetic: none -> 0.82 us  [shards(): table = jnp.concatenate([block_mask, wide_owner], axis=0)]
where the time goes in v4:
time: 47 us; the launch traced here: 46.3 us
  Pallas kernels  42.8 us (91%)
  local copies, waits for them, and re-layouts  2.68 us (6%)
  other arithmetic  0.82 us (2%)
    pallas_call x1, Pallas kernels, shards(): pl.pallas_call(functools.partial(kernel, n_row, n_col), out_shape=jax.Sha...  42.8 us
    unnamed x3, local copies, waits for them, and re-layouts  2.68 us

profile of v4, /device:TPU:9, one launch (start us, length us, event | category | flops | bytes accessed | tf_op | source)
XLA Modules:
  0.0 46.3 jit_solution(5111406721368554391)
XLA Ops:
  0.0 0.8 %pad_add_fusion.table_in = s32[104,96]{1,0:T(8,128)S(1)} fusion(s32[4,8]{1,0:T(4,128)} %param.5, s32[96,96]{1,0:T(8,128)} %param.4), kind=kLoop, calls=%fused_computation | loop fusion | flops 9984 | bytes 76928 | tf_op jit(solution)/shard_map/concatenate | solution.py:358
  0.8 0.0 copy-start
  0.8 1.3 %copy-done = bf16[1536,384]{1,0:T(8,128)(2,1)S(1)} copy-done((bf16[1536,384]{1,0:T(8,128)(2,1)S(1)}, bf16[1536,384]{1,0:T(8,128)(2,1)}, u32[]{:S(2)}) %copy-start) | copy-done | bytes 1179672
  2.1 42.8 %fox.1 = f32[12,128,384]{2,1,0:T(8,128)S(1)} custom-call(bf16[12,128,384]{2,1,0:T(8,128)(2,1)S(1)} %bitcast.3, s32[104,96]{1,0:T(8,128)S(1)} %pad_add_fusion.table_in), custom_call_target="tpu_custom_call" | custom-call | flops 1811939328 | bytes 3538944 | tf_op jit(solution)/shard_map/fox/pallas_call | solution.py:359
  44.9 1.4 %copy.5 = f32[1536,384]{1,0:T(8,128)} copy(f32[1536,384]{1,0:T(8,128)S(1)} %bitcast.2) | data formatting | bytes 4718592
Async XLA Ops:
  0.8 1.3 %copy-start = (bf16[1536,384]{1,0:T(8,128)(2,1)S(1)}, bf16[1536,384]{1,0:T(8,128)(2,1)}, u32[]{:S(2)}) copy-start(bf16[1536,384]{1,0:T(8,128)(2,1)} %param.3) | copy-start | bytes 3538948

commit v5 on v4

--- a/solution.py
+++ b/solution.py
@@ -24,8 +24,8 @@
 
 
 def kernel(
-    n_row, n_col, density, table_in, result,
-    table, tile, nxt, slots, packed, swapped, chosen, crossed, near_0, near_1, near_2, near_3, far_0, far_1, far_2, far_3, r_send, r_all, passing, out,
+    n_row, n_col, density, mask_in, owner_in, result,
+    mask, owner, tile, nxt, slots, packed, swapped, chosen, crossed, near_0, near_1, near_2, near_3, far_0, far_1, far_2, far_3, r_send, r_all, passing, out,
     load_sem, table_sem, swap_s, swap_r, cross_s, cross_r, up_s, down_s, ring_r, mate_s, mate_r, slab_s, slab_r, pass_s, pass_r, out_sem,
 ):
     near, far = (near_0, near_1, near_2, near_3), (far_0, far_1, far_2, far_3)
@@ -39,7 +39,6 @@
     rel = lax.rem(plane - g + planes, planes)
     is_source = rel < STEPS
     row_blocks, _, width = density.shape
-    len_mask = n_col * row_blocks
     col_blocks = width // BLOCK
     my_rows = pl.ds(pl.multiple_of(core * HALF, HALF), HALF)
     mate_rows = pl.ds(pl.multiple_of((1 - core) * HALF, HALF), HALF)
@@ -60,7 +59,10 @@
     for device in senders:
         pl.semaphore_signal(barrier, inc=1, device_id=device, device_id_type=MESH)
 
-    tables = [pltpu.make_async_copy(table_in, table, table_sem.at[0])]
+    tables = [
+        pltpu.make_async_copy(mask_in, mask, table_sem.at[0]),
+        pltpu.make_async_copy(owner_in, owner, table_sem.at[1]),
+    ]
     loads = [
         pltpu.make_async_copy(
             density.at[:, :, pl.ds(b * BLOCK, BLOCK)], tile.at[b, pl.ds(0, row_blocks)], load_sem.at[b]
@@ -83,7 +85,7 @@
     for q in reversed(range(4 * row_blocks)):
         a, b = q // 4, q % 4
         if b < col_blocks:
-            bit = table[g * row_blocks + a, j * col_blocks + b]
+            bit = mask[g * row_blocks + a, j * col_blocks + b]
             first = first + bit * (q - first)
         nxt[q] = first
 
@@ -146,13 +148,13 @@
     def _():
         swap(1).start()
 
-    pick = table[len_mask + jnp.minimum(rel, STEPS - 1), g] & (sub - 1)
+    pick = owner[jnp.minimum(rel, STEPS - 1), g] & (sub - 1)
 
     for t in range(STEPS):
-        slab = (table[len_mask + t, lax.rem(g - t + n_col, n_col)] & (sub - 1)) * col_blocks
+        slab = (owner[t, lax.rem(g - t + n_col, n_col)] & (sub - 1)) * col_blocks
         for a in range(col_blocks):
             for b in range(col_blocks):
-                bit = table[g * row_blocks + slab + a, j * col_blocks + b]
+                bit = mask[g * row_blocks + slab + a, j * col_blocks + b]
                 block = tile[b, row_blocks + bit * (slab + a - row_blocks)]
                 if t == 0:
                     r_all[0, a * BLOCK : (a + 1) * BLOCK, b * BLOCK : (b + 1) * BLOCK] = block
@@ -191,11 +193,11 @@
 
 
     for t in range(STEPS):
-        at = table[len_mask + t, g] * col_blocks
+        at = owner[t, g] * col_blocks
         count = jnp.int32(0)
         for a in range(row_blocks):
             for b in range(col_blocks):
-                bit = table[g * row_blocks + a, at + b]
+                bit = mask[g * row_blocks + a, at + b]
                 slots[t, a * col_blocks + b] = CAP + bit * (count - CAP)
                 count = count + bit
     out[...] = jnp.zeros_like(out)
@@ -354,15 +356,18 @@
     dma = pltpu.SemaphoreType.DMA
     bf16 = jnp.bfloat16
     piece = (CAP, HALF, BLOCK)
-    wide_owner = jnp.pad(owner, ((0, 8 - owner.shape[0]), (0, block_mask.shape[1] - owner.shape[1])))
-    table = jnp.concatenate([block_mask, wide_owner], axis=0)
+    operands = [
+        pltpu.with_memory_space_constraint(operand, pltpu.HBM)
+        for operand in (density.reshape(row_blocks, BLOCK, width), block_mask, owner)
+    ]
     return pl.pallas_call(
         functools.partial(kernel, n_row, n_col),
         out_shape=jax.ShapeDtypeStruct((row_blocks, BLOCK, width), jnp.float32),
-        in_specs=[pl.BlockSpec(memory_space=pltpu.HBM)] * 2,
+        in_specs=[pl.BlockSpec(memory_space=pltpu.HBM)] * 3,
         out_specs=pl.BlockSpec(memory_space=pl.ANY),
         scratch_shapes=[
-            pltpu.SMEM(table.shape, jnp.int32),
+            pltpu.SMEM(block_mask.shape, jnp.int32),
+            pltpu.SMEM(owner.shape, jnp.int32),
             pltpu.VMEM((col_blocks, row_blocks + 1, BLOCK, BLOCK), bf16),
             pltpu.SMEM((4 * row_blocks + 1,), jnp.int32),
             pltpu.SMEM((STEPS, row_blocks * col_blocks), jnp.int32),
@@ -387,7 +392,7 @@
             flops=2 * rows * width * width * STEPS, bytes_accessed=rows * width * 6, transcendentals=0
         ),
         name="fox",
-    )(density.reshape(row_blocks, BLOCK, width), table).reshape(rows, width)
+    )(*operands).reshape(rows, width)
 
 
 def solution(mesh):

time: 47 us -> 45 us (0.957)
  local copies, waits for them, and re-layouts: 2.68 us -> 1.41 us
  other arithmetic: 0.82 us -> 0 us
    unnamed x3 -> x1, local copies, waits for them, and re-layouts: 2.68 us -> 1.41 us
    concatenate x1 -> x0, other arithmetic: 0.82 us -> none  [shards(): table = jnp.concatenate([block_mask, wide_owner], axis=0)]
where the time goes in v5:
time: 45 us; the launch traced here: 44.5 us
  Pallas kernels  43 us (96%)
  local copies, waits for them, and re-layouts  1.41 us (3%)
    pallas_call x1, Pallas kernels, shards(): pl.pallas_call(functools.partial(kernel, n_row, n_col), out_shape=jax.Sha...  43 us
    unnamed x1, local copies, waits for them, and re-layouts  1.41 us

profile of v5, /device:TPU:9, one launch (start us, length us, event | category | flops | bytes accessed | tf_op | source)
XLA Modules:
  0.0 44.5 jit_solution(11483535823882058789)
XLA Ops:
  0.0 43.0 %fox.1 = f32[12,128,384]{2,1,0:T(8,128)S(1)} custom-call(bf16[12,128,384]{2,1,0:T(8,128)(2,1)} %bitcast.3, s32[96,96]{1,0:T(8,128)} %mask_in.1, s32[4,8]{1,0:T(4,128)} %owner_in.1), custom_call_target="tpu_custom_call" | custom-call | flops 1811939328 | bytes 3538944 | tf_op jit(solution)/shard_map/fox/pallas_call | solution.py:363
  43.1 1.4 %copy.5 = f32[1536,384]{1,0:T(8,128)} copy(f32[1536,384]{1,0:T(8,128)S(1)} %bitcast.2) | data formatting | bytes 4718592

commit v6 on v5

--- a/solution.py
+++ b/solution.py
@@ -14,7 +14,7 @@
 CHUNKS = 7
 SPAN = CAP // CHUNKS
 LAG = 4
-SHIFT = 3
+SHIFT = 4
 AFTER = 2
 DETOUR = 12
 READY = 17

time: 45 us -> 44.8 us (level)
  no operation moved by 1% of the time
where the time goes in v6:
time: 44.8 us; the launch traced here: 44.6 us
  Pallas kernels  43.2 us (96%)
  local copies, waits for them, and re-layouts  1.41 us (3%)
    pallas_call x1, Pallas kernels, shards(): pl.pallas_call(functools.partial(kernel, n_row, n_col), out_shape=jax.Sha...  43.2 us
    unnamed x1, local copies, waits for them, and re-layouts  1.41 us

profile of v6, /device:TPU:9, one launch (start us, length us, event | category | flops | bytes accessed | tf_op | source)
XLA Modules:
  0.0 44.6 jit_solution(2855874017241254778)
XLA Ops:
  0.0 43.2 %fox.1 = f32[12,128,384]{2,1,0:T(8,128)S(1)} custom-call(bf16[12,128,384]{2,1,0:T(8,128)(2,1)} %bitcast.3, s32[96,96]{1,0:T(8,128)} %mask_in.1, s32[4,8]{1,0:T(4,128)} %owner_in.1), custom_call_target="tpu_custom_call" | custom-call | flops 1811939328 | bytes 3538944 | tf_op jit(solution)/shard_map/fox/pallas_call | solution.py:363
  43.2 1.4 %copy.5 = f32[1536,384]{1,0:T(8,128)} copy(f32[1536,384]{1,0:T(8,128)S(1)} %bitcast.2) | data formatting | bytes 4718592

commit v7 on v6

--- a/solution.py
+++ b/solution.py
@@ -15,9 +15,9 @@
 SPAN = CAP // CHUNKS
 LAG = 4
 SHIFT = 4
-AFTER = 2
+AFTER = 3
 DETOUR = 12
-READY = 17
+READY = 18
 UNITS = 4
 UP = (3, 3, 4, 4)
 MESH = pl.DeviceIdType.MESH

time: 44.8 us -> 44.4 us (level)
  Pallas kernels: 43.2 us -> 42.7 us
    pallas_call x1, Pallas kernels: 43.2 us -> 42.7 us  [shards(): pl.pallas_call(functools.partial(kernel, n_row, n_col), out_shape=jax.Sha...]
where the time goes in v7:
time: 44.4 us; the launch traced here: 44.1 us
  Pallas kernels  42.7 us (96%)
  local copies, waits for them, and re-layouts  1.41 us (3%)
    pallas_call x1, Pallas kernels, shards(): pl.pallas_call(functools.partial(kernel, n_row, n_col), out_shape=jax.Sha...  42.7 us
    unnamed x1, local copies, waits for them, and re-layouts  1.41 us

profile of v7, /device:TPU:9, one launch (start us, length us, event | category | flops | bytes accessed | tf_op | source)
XLA Modules:
  0.0 44.1 jit_solution(11270076773239522789)
XLA Ops:
  0.0 42.7 %fox.1 = f32[12,128,384]{2,1,0:T(8,128)S(1)} custom-call(bf16[12,128,384]{2,1,0:T(8,128)(2,1)} %bitcast.3, s32[96,96]{1,0:T(8,128)} %mask_in.1, s32[4,8]{1,0:T(4,128)} %owner_in.1), custom_call_target="tpu_custom_call" | custom-call | flops 1811939328 | bytes 3538944 | tf_op jit(solution)/shard_map/fox/pallas_call | solution.py:363
  42.7 1.4 %copy.5 = f32[1536,384]{1,0:T(8,128)} copy(f32[1536,384]{1,0:T(8,128)S(1)} %bitcast.2) | data formatting | bytes 4718592
